TPU v7x, 512 devices: a whole 4x8x8 slice. The times are simulated.
512 devices in a mesh: lon: 16 (over z, core), lat: 32 (over y, x).
Axes of the slice: x: 4, y: 8, z: 8, core: 2. Of those that a mesh axis runs over, the one named last changes fastest.
Arguments:
- increment: float32 [2, 64, 768, 2048], P(None, None, 'lat', 'lon'), may hold values from -6 to 6
- eastward_rate: float32 [2, 64, 768], P(None, None, 'lat'), as said below
- eastward_spike: float32 [768, 2048], P('lat', 'lon'), as said below
- northward_rate: float32 [2, 64, 768], replicated, as said below
- vertical: float32 [2, 64, 64], replicated, may hold values from -0.75 to 0.75
Outputs:
- correlated: float32 [2, 64, 768, 2048], P(None, None, 'lat', 'lon')
Inputs may be any that keep to these rules, and one draw needn't show every extreme that they name: `eastward_rate`: every entry is positive and below 1. `eastward_spike`: every entry is positive and at most 1. `northward_rate`: every entry is positive and below 1.
All inputs are finite; a program needn't handle non-finite values.
Results may differ from a plain program's by a relative error of at most 0.0003.
Values sent between devices are 32-bit elements; how exact they have to be, the bound alone decides.
A program may use at most 64 MiB of HBM per device.

v0:
```python
import jax
import jax.numpy as jnp
from jax import lax
from jax.sharding import PartitionSpec as P


def carried_in(x, axis, combine, identity):
    length, mine = (lax.axis_size(axis), lax.axis_index(axis))
    everything = jax.tree.map(lambda part: lax.all_gather(part, axis), x)
    start = jax.tree.map(
        lambda part, zero: jnp.broadcast_to(jnp.asarray(zero, part.dtype), part.shape), x, identity
    )

    def lap(k, before):
        at = length - 1 - k
        reached = at > mine
        new = combine(before, jax.tree.map(lambda part: part[at], everything))
        return jax.tree.map(lambda a, b: jnp.where(reached, a, b), new, before)

    return lax.fori_loop(0, length, lap, start)


def from_root(block, axis, source):
    block = jnp.where(lax.axis_index(axis) == source, block, jnp.zeros_like(block))
    return lax.psum(block, axis)


def compose(earlier, following):
    return (following[0] * earlier[0], following[1] + following[0] * earlier[1])


def matmul_last(values, matrix):
    flat = values.reshape((-1, values.shape[-1]))
    result = jnp.dot(
        flat, matrix, precision=lax.Precision.HIGHEST, preferred_element_type=jnp.float32
    )
    return result.reshape(values.shape[:-1] + (matrix.shape[1],))


def row_filter(rates):
    length = rates.shape[-1]
    totals = jnp.cumsum(jnp.log(rates), axis=-1)
    upper = lax.broadcasted_iota(jnp.int32, (length, length), 0)
    lower = lax.broadcasted_iota(jnp.int32, (length, length), 1)
    keeping = lower <= upper
    spread = totals[..., :, None] - totals[..., None, :]
    weights = jnp.where(keeping, jnp.exp(jnp.where(keeping, spread, -60.0)), 0.0)
    return (weights, jnp.exp(totals))


def shards(increment, eastward_rate, eastward_spike, northward_rate, vertical):
    lon_cols = increment.shape[3]
    decay_factors = eastward_rate[:, :, :, None] * eastward_spike[None, None, :, :]
    row_index = lax.broadcasted_iota(jnp.int32, (lon_cols, lon_cols), 0)
    col_index = lax.broadcasted_iota(jnp.int32, (lon_cols, lon_cols), 1)
    before_mat = (row_index < col_index).astype(jnp.float32)
    suffix_mat = (row_index >= col_index).astype(jnp.float32)
    log_decay = jnp.log(decay_factors)
    prefix_log = matmul_last(log_decay, before_mat)
    total_log = jnp.sum(log_decay, axis=3)
    suffix_sums = matmul_last(jnp.exp(prefix_log) * increment, suffix_mat)
    local_part = jnp.exp(-prefix_log) * suffix_sums
    factor = jnp.exp(total_log[:, :, :, None] - prefix_log)
    block_factor = jnp.exp(total_log)
    block_local = local_part[:, :, :, 0]
    identity_map = (jnp.ones_like(block_factor), jnp.zeros_like(block_local))
    after_factor, after_local = carried_in(
        (block_factor, block_local), "lon", compose, identity_map
    )
    whole_factor, whole_local = compose((after_factor, after_local), (block_factor, block_local))
    shared = from_root(jnp.stack([whole_factor, whole_local]), "lon", 0)
    loop_factor = shared[0]
    loop_local = shared[1]
    wrapped = loop_local / (1.0 - loop_factor)
    incoming = after_local + after_factor * wrapped
    eastward_output = jnp.sqrt(1.0 - decay_factors * decay_factors) * (
        local_part + factor * incoming[:, :, :, None]
    )
    columns = lax.all_to_all(eastward_output, "lat", split_axis=1, concat_axis=2, tiled=True)
    levels_here = columns.shape[1]
    first_level = lax.axis_index("lat") * levels_here
    row_rates = lax.dynamic_slice_in_dim(northward_rate, first_level, levels_here, 1)
    weights, growth = row_filter(row_rates)
    filtered = jnp.einsum("vljk,vlki->vlji", weights, columns, precision=lax.Precision.HIGHEST)
    scaled = jnp.sqrt(1.0 - row_rates * row_rates)[:, :, :, None] * filtered
    meridional_out = lax.all_to_all(scaled, "lat", split_axis=2, concat_axis=1, tiled=True)
    return jnp.einsum("vlk,vlab->vkab", vertical, meridional_out, precision=lax.Precision.HIGHEST)


def solution(mesh):
    return jax.shard_map(
        shards,
        mesh=mesh,
        in_specs=(P(None, None, "lat", "lon"), P(None, None, "lat"), P("lat", "lon"), P(), P()),
        out_specs=P(None, None, "lat", "lon"),
        check_vma=False,
    )
```

profile of v0, /device:TPU:192, one launch (start us, length us, event | category | flops | bytes accessed | tf_op | source)
XLA Modules:
  0.0 217.6 jit_solution(4784289971304212418)
XLA Ops:
  0.0 0.0 copy-start
  0.0 0.0 copy-start.1
  0.0 0.9 copy.57
  0.9 1.7 fusion.12
  2.6 0.0 copy-done.1
  2.6 0.9 fusion.11
  3.5 2.4 %exponential_multiply_fusion = f32[2,64,24,128]{3,2,1,0:T(8,128)S(1)} fusion(f32[2,64,24,128]{3,2,1,0:T(8,128)S(1)} %fusion.12, f32[2,64,24,128]{3,2,1,0:T(8,128)} %param.7), kind=kOutput, calls=%fused_computation.25 | convolution fusion | flops 605175808 | bytes 4718592 | tf_op jit(solution)/shard_map/dot_general | solution.py:34
  6.0 0.5 copy.59
  6.5 19.0 %all-gather.1 = f32[32,64,24,1]{1,2,3,0:T(8,128)} all-gather(f32[2,64,24,1]{1,2,3,0:T(8,128)S(1)} %copy.59), channel_id=3, replica_groups=mesh['lon'=16,'lat'=32] {'lon'}, dimensions={0}, use_global_device_ids=true | all-gather | bytes 208896 | tf_op jit(solution)/shard_map/all_gather | solution.py:9
  25.5 0.1 copy.58
  25.6 19.0 %all-gather = f32[32,64,24]{1,2,0:T(8,128)} all-gather(f32[2,64,24]{1,2,0:T(8,128)S(1)} %exp.29), channel_id=2, replica_groups=mesh['lon'=16,'lat'=32] {'lon'}, dimensions={0}, use_global_device_ids=true | all-gather | bytes 208896 | tf_op jit(solution)/shard_map/all_gather | solution.py:9
  44.6 12.8 %while.18 = (s32[]{:T(128)}, f32[2,64,24]{1,2,0:T(8,128)S(1)}, f32[2,64,24]{1,2,0:T(8,128)S(1)}, s32[]{:T(128)}, f32[16,2,64,24]{2,3,1,0:T(8,128)}, /*index=5*/f...) while((s32[]{:T(128)}, f32[2,64,24]{1,2,0:T(8,128)S(1)}, ...), condition=%wide.region_4.5_spmd.clone, body=%wide.region_3.4_spmd.clone.sunk | while | flops 21512 | bytes 73899 | solution.py:20
  44.6 0.8 fusion.41
  45.4 0.8 fusion.41
  46.2 0.8 fusion.41
  47.0 0.8 fusion.41
  47.8 0.8 fusion.41
  48.6 0.8 fusion.41
  49.4 0.8 fusion.41
  50.2 0.8 fusion.41
  51.0 0.8 fusion.41
  51.8 0.8 fusion.41
  52.6 0.8 fusion.41
  53.4 0.8 fusion.41
  54.2 0.8 fusion.41
  55.0 0.8 fusion.41
  55.8 0.8 fusion.41
  56.6 0.8 fusion.41
  57.4 44.1 %psum.7 = f32[2,2,64,24]{2,3,1,0:T(8,128)S(1)} all-reduce(f32[2,2,64,24]{2,3,1,0:T(8,128)S(1)} %maximum_select_fusion), channel_id=1, replica_groups=mesh['lon'=16,'lat'=32] {'lon'}, use_global_device_ids=true, to_apply=%region_5.6 | all-reduce | flops 6144 | bytes 49152 | tf_op jit(solution)/shard_map/psum | solution.py:25
  101.6 0.1 copy.61
  101.6 1.5 fusion.15
  103.2 1.3 copy.62
  104.5 9.9 %all-to-all-start = ((f32[2,64,24,128]{3,2,0,1:T(8,128)}), f32[2,64,24,128]{3,2,0,1:T(8,128)S(1)}, u32[]{:S(2)}, u32[]{:S(2)}) async-start(f32[2,64,24,128]{3,2,0,1:T(8,128)} %copy.62), calls=%async_computation | async-start | bytes 3145728 | tf_op jit(solution)/shard_map/all_to_all | solution.py:79
  114.4 0.8 subtract_sqrt_fusion
  115.3 1.2 reduce-window.6
  116.4 0.2 slice_reduce_fusion
  116.6 0.4 reduce-window.9
  117.0 0.1 broadcast_add_fusion
  117.1 0.2 iota_compare_fusion
  117.3 37.2 %all-to-all-done = f32[2,64,24,128]{3,2,0,1:T(8,128)S(1)} async-done(((f32[2,64,24,128]{3,2,0,1:T(8,128)}), f32[2,64,24,128]{3,2,0,1:T(8,128)S(1)}, u32[]{:S(2)}, u32[]{:S(2)}) %all-to-all-start) | async-done | bytes 1572896 | tf_op jit(solution)/shard_map/all_to_all | solution.py:79
  154.5 0.1 copy.63
  154.6 10.2 %fusion.21 = f32[2,2,768,128]{3,2,1,0:T(8,128)S(1)} fusion(f32[2,2,768,128]{3,2,1,0:T(8,128)S(1)} %bitcast.62, f32[2,2,768]{2,1,0:T(2,128)S(1)} %reduce_window_sum.23, pred[768,768]{1,0:T(8,128)(4,1)S(1)} %iota_compare_fusion, f32[2,2,768]{2,1,0:T(2,128)S(1)} %get-tuple-element.203), kind=kOutput, calls=%fused_computation.27 | convolution fusion | flops 3631349760 | bytes 3760128 | tf_op jit(solution)/shard_map/vljk,vlki->vlji/dot_general | solution.py:84
  164.8 1.4 copy.64
  166.3 46.9 %all_to_all.36 = f32[2,2,768,128]{3,1,0,2:T(2,128)S(1)} all-to-all(f32[2,2,768,128]{3,1,0,2:T(2,128)S(1)} %copy.64), channel_id=1, replica_groups=mesh['lon'=16,'lat'=32] {'lat'}, dimensions={2} | all-to-all | bytes 3145728 | tf_op jit(solution)/shard_map/all_to_all | solution.py:86
  213.1 0.9 copy.65
  214.0 0.0 copy-done
  214.0 1.5 convolution_bitcast_fusion
  215.5 2.1 copy.67
  (8 shorter events, 0.1 us)
Async XLA Ops:
  0.0 214.0 %copy-start = (f32[2,64,64]{2,1,0:T(8,128)S(1)}, f32[2,64,64]{2,1,0:T(8,128)}, u32[]{:S(2)}) copy-start(f32[2,64,64]{2,1,0:T(8,128)} %param.11) | copy-start | bytes 98308
  0.0 2.6 %copy-start.1 = (f32[24,128]{1,0:T(8,128)S(1)}, f32[24,128]{1,0:T(8,128)}, u32[]{:S(2)}) copy-start(f32[24,128]{1,0:T(8,128)} %param.9) | copy-start | bytes 36868
  104.5 50.1 %all-to-all-start = ((f32[2,64,24,128]{3,2,0,1:T(8,128)}), f32[2,64,24,128]{3,2,0,1:T(8,128)S(1)}, u32[]{:S(2)}, u32[]{:S(2)}) async-start(f32[2,64,24,128]{3,2,0,1:T(8,128)} %copy.62), calls=%async_computation | async-start | bytes 3145728 | tf_op jit(solution)/shard_map/all_to_all | solution.py:79
where the time goes:
time: 219 us; the launch traced here: 218 us
  blocking collectives  129 us (59%)
  waiting for transfers between devices  37.2 us (17%)
  other arithmetic  17.5 us (8%)
  matrix products  15.8 us (7%)
  starting transfers between devices  9.95 us (5%)
  local copies, waits for them, and re-layouts  7.5 us (3%)
    all_to_all x1, blocking collectives, shards(): lax.all_to_all(scaled, 'lat', split_axis=2, concat_axis=1, tiled=True)  46.9 us
    psum x1, blocking collectives, from_root(): return lax.psum(block, axis)  44.1 us
    all_gather x2, blocking collectives, carried_in(): everything = jax.tree.map(lambda part: lax.all_gather(part, axis), x)  37.9 us
    all_to_all x1, waiting for transfers between devices, shards(): lax.all_to_all(eastward_output, 'lat', split_axis=1, concat_axis=2, tiled...  37.2 us
    select_n x16, other arithmetic, lap(): return jax.tree.map(lambda a, b: jnp.where(reached, a, b), new, before)  12.4 us
    dot_general x1, matrix products, shards(): jnp.einsum('vljk,vlki->vlji', weights, columns, precision=lax.Precision.H...  10.2 us
    all_to_all x1, starting transfers between devices, shards(): lax.all_to_all(eastward_output, 'lat', split_axis=1, concat_axis=2, tiled...  9.95 us
  transfers between devices with their start and end apart: 1, of which 1 were waited for; matrix products, arithmetic and copies ran while one was open for 1% of the time, Pallas kernels for 0%

commit v1 on v0

--- a/solution.py
+++ b/solution.py
@@ -2,6 +2,12 @@
 import jax.numpy as jnp
 from jax import lax
 from jax.sharding import PartitionSpec as P
+
+
+def _review_sheets(my_data, chip_axis):
+    state_next = jnp.stack(jnp.split(my_data, lax.axis_size(chip_axis), 2))
+    kept_arr = lax.all_to_all(state_next, axis_name=chip_axis, split_axis=0, concat_axis=0)
+    return jnp.concatenate(kept_arr, 1)
 
 
 def carried_in(x, axis, combine, identity):
@@ -83,7 +89,7 @@
     weights, growth = row_filter(row_rates)
     filtered = jnp.einsum("vljk,vlki->vlji", weights, columns, precision=lax.Precision.HIGHEST)
     scaled = jnp.sqrt(1.0 - row_rates * row_rates)[:, :, :, None] * filtered
-    meridional_out = lax.all_to_all(scaled, "lat", split_axis=2, concat_axis=1, tiled=True)
+    meridional_out = _review_sheets(scaled, "lat")
     return jnp.einsum("vlk,vlab->vkab", vertical, meridional_out, precision=lax.Precision.HIGHEST)
 
 

time: 219 us -> 218 us (level)
  the two profiles are of different devices: /device:TPU:192 before, /device:TPU:8 now
where the time goes in v1:
time: 218 us; the launch traced here: 217 us
  blocking collectives  133 us (61%)
  waiting for transfers between devices  31.9 us (15%)
  other arithmetic  18.2 us (8%)
  matrix products  15.9 us (7%)
  starting transfers between devices  10.2 us (5%)
  local copies, waits for them, and re-layouts  6.46 us (3%)
    psum x1, blocking collectives, from_root(): return lax.psum(block, axis)  47.3 us
    all_to_all x1, blocking collectives, _review_sheets(): lax.all_to_all(state_next, axis_name=chip_axis, split_axis=0, concat_axis=0)  43.2 us
    all_gather x2, blocking collectives, carried_in(): everything = jax.tree.map(lambda part: lax.all_gather(part, axis), x)  42.6 us
    all_to_all x1, waiting for transfers between devices, shards(): lax.all_to_all(eastward_output, 'lat', split_axis=1, concat_axis=2, tiled...  31.9 us
    select_n x16, other arithmetic, lap(): return jax.tree.map(lambda a, b: jnp.where(reached, a, b), new, before)  12.4 us
    all_to_all x1, starting transfers between devices, shards(): lax.all_to_all(eastward_output, 'lat', split_axis=1, concat_axis=2, tiled...  10.2 us
    dot_general x1, matrix products, shards(): jnp.einsum('vljk,vlki->vlji', weights, columns, precision=lax.Precision.H...  10 us
  transfers between devices with their start and end apart: 1, of which 1 were waited for; matrix products, arithmetic and copies ran while one was open for 2% of the time, Pallas kernels for 0%

profile of v1, /device:TPU:8, one launch (start us, length us, event | category | flops | bytes accessed | tf_op | source)
XLA Modules:
  0.0 216.6 jit_solution(8549013409714084407)
XLA Ops:
  0.0 0.0 copy-start
  0.0 0.0 copy-start.2
  0.0 0.9 copy.57
  0.9 1.7 fusion.12
  2.6 0.0 copy-done.2
  2.6 0.9 fusion.11
  3.5 2.4 %exponential_multiply_fusion = f32[2,64,24,128]{3,2,1,0:T(8,128)S(1)} fusion(f32[2,64,24,128]{3,2,1,0:T(8,128)S(1)} %fusion.12, f32[2,64,24,128]{3,2,1,0:T(8,128)} %param.7), kind=kOutput, calls=%fused_computation.27 | convolution fusion | flops 605175808 | bytes 4718592 | tf_op jit(solution)/shard_map/dot_general | solution.py:40
  6.0 0.5 copy.59
  6.5 25.6 %all-gather.1 = f32[32,64,24,1]{1,2,3,0:T(8,128)} all-gather(f32[2,64,24,1]{1,2,3,0:T(8,128)S(1)} %copy.59), channel_id=3, replica_groups=mesh['lon'=16,'lat'=32] {'lon'}, dimensions={0}, use_global_device_ids=true | all-gather | bytes 208896 | tf_op jit(solution)/shard_map/all_gather | solution.py:15
  32.1 0.1 copy.58
  32.2 16.9 %all-gather = f32[32,64,24]{1,2,0:T(8,128)} all-gather(f32[2,64,24]{1,2,0:T(8,128)S(1)} %exp.29), channel_id=2, replica_groups=mesh['lon'=16,'lat'=32] {'lon'}, dimensions={0}, use_global_device_ids=true | all-gather | bytes 208896 | tf_op jit(solution)/shard_map/all_gather | solution.py:15
  49.2 12.8 %while.18 = (s32[]{:T(128)}, f32[2,64,24]{1,2,0:T(8,128)S(1)}, f32[2,64,24]{1,2,0:T(8,128)S(1)}, s32[]{:T(128)}, f32[16,2,64,24]{2,3,1,0:T(8,128)}, /*index=5*/f...) while((s32[]{:T(128)}, f32[2,64,24]{1,2,0:T(8,128)S(1)}, ...), condition=%wide.region_4.5_spmd.clone, body=%wide.region_3.4_spmd.clone.sunk | while | flops 21512 | bytes 73899 | solution.py:26
  49.2 0.8 fusion.45
  50.0 0.8 fusion.45
  50.8 0.8 fusion.45
  51.6 0.8 fusion.45
  52.4 0.8 fusion.45
  53.2 0.8 fusion.45
  54.0 0.8 fusion.45
  54.8 0.8 fusion.45
  55.6 0.8 fusion.45
  56.4 0.8 fusion.45
  57.2 0.8 fusion.45
  58.0 0.8 fusion.45
  58.8 0.8 fusion.45
  59.6 0.8 fusion.45
  60.4 0.8 fusion.45
  61.2 0.8 fusion.45
  62.0 47.3 %psum.7 = f32[2,2,64,24]{2,3,1,0:T(8,128)S(1)} all-reduce(f32[2,2,64,24]{2,3,1,0:T(8,128)S(1)} %maximum_select_fusion), channel_id=1, replica_groups=mesh['lon'=16,'lat'=32] {'lon'}, use_global_device_ids=true, to_apply=%region_5.6 | all-reduce | flops 6144 | bytes 49152 | tf_op jit(solution)/shard_map/psum | solution.py:31
  109.3 0.1 copy.61
  109.4 1.5 fusion.15
  111.0 1.3 copy.62
  112.2 10.2 %all-to-all-start = ((f32[2,64,24,128]{3,2,0,1:T(8,128)}), f32[2,64,24,128]{3,2,0,1:T(8,128)S(1)}, u32[]{:S(2)}, u32[]{:S(2)}) async-start(f32[2,64,24,128]{3,2,0,1:T(8,128)} %copy.62), calls=%async_computation | async-start | bytes 3145728 | tf_op jit(solution)/shard_map/all_to_all | solution.py:85
  122.4 0.8 subtract_sqrt_fusion
  123.3 1.2 reduce-window.6
  124.4 0.2 slice_reduce_fusion
  124.6 0.4 reduce-window.9
  124.9 0.1 broadcast_add_fusion
  125.0 1.0 iota_compare_fusion
  126.0 31.9 %all-to-all-done = f32[2,64,24,128]{3,2,0,1:T(8,128)S(1)} async-done(((f32[2,64,24,128]{3,2,0,1:T(8,128)}), f32[2,64,24,128]{3,2,0,1:T(8,128)S(1)}, u32[]{:S(2)}, u32[]{:S(2)}) %all-to-all-start) | async-done | bytes 1572896 | tf_op jit(solution)/shard_map/all_to_all | solution.py:85
  158.0 0.1 copy.63
  158.1 1.0 copy-done.1
  159.0 10.0 %fusion.26 = f32[2,2,768,128]{3,2,1,0:T(8,128)S(1)} fusion(f32[2,2,768,128]{3,2,1,0:T(8,128)S(1)} %bitcast.187, f32[2,2,768]{2,1,0:T(2,128)S(1)} %reduce_window_sum.23, pred[768,768]{1,0:T(8,128)(4,1)S(1)} %copy-done.1, f32[2,2,768]{2,1,0:T(2,128)S(1)} %get-tuple-element.203), kind=kOutput, calls=%fused_computation.29 | convolution fusion | flops 3631349760 | bytes 3760128 | tf_op jit(solution)/shard_map/vljk,vlki->vlji/dot_general | solution.py:90
  169.5 43.2 %all_to_all.23 = f32[32,2,2,24,128]{4,3,2,1,0:T(8,128)S(1)} all-to-all(f32[32,2,2,24,128]{4,3,2,1,0:T(8,128)S(1)} %constant_dynamic-update-slice_fusion), channel_id=1, replica_groups=mesh['lon'=16,'lat'=32] {'lat'}, dimensions={0} | all-to-all | bytes 3145728 | tf_op jit(solution)/shard_map/all_to_all | solution.py:9
  212.7 0.1 copy.64
  212.8 0.0 copy-done
  212.8 1.7 fusion.21
  214.5 2.1 copy.67
  (41 shorter events, 0.3 us)
Async XLA Ops:
  0.0 212.8 %copy-start = (f32[2,64,64]{2,1,0:T(8,128)S(1)}, f32[2,64,64]{2,1,0:T(8,128)}, u32[]{:S(2)}) copy-start(f32[2,64,64]{2,1,0:T(8,128)} %param.11) | copy-start | bytes 98308
  0.0 2.6 %copy-start.2 = (f32[24,128]{1,0:T(8,128)S(1)}, f32[24,128]{1,0:T(8,128)}, u32[]{:S(2)}) copy-start(f32[24,128]{1,0:T(8,128)} %param.9) | copy-start | bytes 36868
  112.2 45.7 %all-to-all-start = ((f32[2,64,24,128]{3,2,0,1:T(8,128)}), f32[2,64,24,128]{3,2,0,1:T(8,128)S(1)}, u32[]{:S(2)}, u32[]{:S(2)}) async-start(f32[2,64,24,128]{3,2,0,1:T(8,128)} %copy.62), calls=%async_computation | async-start | bytes 3145728 | tf_op jit(solution)/shard_map/all_to_all | solution.py:85
  158.0 1.1 copy-start.1
